TPU v7x, 512 devices: a whole 4x8x8 slice. The times are simulated.
512 devices in a mesh: tm: 16 (over y, core), nin: 8 (over z), nout: 4 (over x).
Axes of the slice: x: 4, y: 8, z: 8, core: 2. Of those that a mesh axis runs over, the one named last changes fastest.
Arguments:
- spikes: int32 [4096, 2048], P('tm', 'nin'), may hold values 0 or 1
- exposure: int32 [4096], P('tm'), may hold values from 1 to 8
- weights: bfloat16 [16384, 2048], P('nin', 'nout'), may hold values from -0.375 to 0.375
- direction: float32 [16384, 2048], P(('nin', 'tm'), 'nout'), may hold values from -6 to 6
- residual: float32 [16384, 2048], P(('nin', 'tm'), 'nout'), may hold values from -0.75 to 0.75
- iterate: float32 [16384, 2048], P(('nin', 'tm'), 'nout'), may hold values from -1.8 to 1.8
Outputs:
- new_iterate: float32 [16384, 2048], P(('nin', 'tm'), 'nout')
- new_residual: float32 [16384, 2048], P(('nin', 'tm'), 'nout')
- new_direction: float32 [16384, 2048], P(('nin', 'tm'), 'nout')
All inputs are finite; a program needn't handle non-finite values. No bound on the sum of `spikes` on one device may be relied on, other than what follows from the above.
Results may differ from a plain program's by a relative error of at most 0.015.
Values may be sent and summed in bfloat16 or wider, within the bound.
A program may use at most 64 MiB of HBM per device.

v0:
```python
import math
import jax
import jax.numpy as jnp
from jax import lax
from jax.sharding import PartitionSpec as P

BASES = 8
HISTORY = 128
RIDGE_WEIGHT = 0.05
NORM_EPS = 1e-06


def shifted(value, axis, steps):
    count = lax.axis_size(axis)
    initial, last = (max(0, -steps), min(count, count - steps))
    return lax.ppermute(value, axis, [(source, source + steps) for source in range(initial, last)])


def basis_table(history, bases_count):
    lag_values = jnp.arange(1, history + 1, dtype=jnp.float32)
    warped = jnp.log(lag_values + 1.0)
    log_low = math.log(2.0)
    log_high = math.log(history + 1.0)
    spacing = (log_high - log_low) / (bases_count - 1)
    centers = log_low + spacing * jnp.arange(bases_count, dtype=jnp.float32)
    phases = (warped[:, None] - centers[None, :]) * (math.pi / (2.0 * spacing))
    phases = jnp.clip(phases, -math.pi, math.pi)
    bump_values = 0.5 * (1.0 + jnp.cos(phases))
    bump_values = bump_values / jnp.sum(bump_values, axis=0, keepdims=True)
    return bump_values.astype(jnp.bfloat16)


def lag_kernel(basis_rows, span, offset):
    out_index = jnp.arange(span, dtype=jnp.int32)[:, None]
    in_index = jnp.arange(span, dtype=jnp.int32)[None, :]
    lag_index = out_index + offset - in_index
    is_valid = (lag_index >= 1) & (lag_index <= HISTORY)
    take_index = jnp.clip(lag_index - 1, 0, HISTORY - 1)
    return jnp.where(
        is_valid[None], jnp.take(basis_rows.T, take_index, axis=1), jnp.zeros((), jnp.bfloat16)
    )


def per_device(spikes, exposure, weights, direction, residual, iterate):
    block_rows = spikes.shape[0]
    neuron_cols = spikes.shape[1]
    basis_rows = basis_table(HISTORY, BASES)
    spike_low = spikes.astype(jnp.bfloat16)
    block_count = block_rows // HISTORY
    stacked = spike_low.reshape(block_count, HISTORY, neuron_cols)
    kernel_same = lag_kernel(basis_rows, HISTORY, 0)
    kernel_before = lag_kernel(basis_rows, HISTORY, HISTORY)
    current = jnp.einsum("bim,cmn->cinb", kernel_same, stacked, preferred_element_type=jnp.float32)
    tail_part = jnp.einsum(
        "bim,mn->inb", kernel_before, stacked[-1], preferred_element_type=jnp.float32
    )
    inner_part = jnp.einsum(
        "bim,cmn->cinb", kernel_before, stacked[:-1], preferred_element_type=jnp.float32
    )
    tail_terms = shifted(tail_part.astype(jnp.bfloat16), "tm", 1).astype(tail_part.dtype)
    own_terms = current + jnp.concatenate([tail_terms[None], inner_part], axis=0)
    features = own_terms.reshape(block_rows, neuron_cols * BASES).astype(jnp.bfloat16)
    direction_low = direction.astype(jnp.bfloat16)
    columns = features
    along_part = jnp.dot(
        columns,
        lax.all_gather(direction_low, "tm", axis=0, tiled=True),
        preferred_element_type=jnp.float32,
    )
    predictor_part = jnp.dot(features, weights, preferred_element_type=jnp.float32)
    tick_scale = exposure.astype(jnp.float32) / 8.0
    predictor_full, along_full = (
        lax.psum(predictor_part.astype(jnp.bfloat16), "nin").astype(jnp.float32),
        lax.psum(along_part.astype(jnp.bfloat16), "nin").astype(jnp.float32),
    )
    weighted = (tick_scale[:, None] * jnp.exp(predictor_full) * along_full).astype(jnp.bfloat16)
    columns = features
    gram = lax.psum_scatter(
        lax.dot_general(
            columns, weighted, (((0,), (0,)), ((), ())), preferred_element_type=jnp.float32
        ).astype(jnp.bfloat16),
        "tm",
        scatter_dimension=0,
        tiled=True,
    ).astype(jnp.float32)
    bin_total = block_rows * lax.axis_size("tm")
    curvature_prod = gram / bin_total + RIDGE_WEIGHT * direction
    old_norm, curvature = lax.psum(
        (jnp.sum(residual * residual, axis=0), jnp.sum(direction * curvature_prod, axis=0)),
        ("tm", "nin"),
    )
    step_size = old_norm / curvature
    new_iterate = iterate + step_size[None, :] * direction
    new_residual = residual - step_size[None, :] * curvature_prod
    new_norm = lax.psum(jnp.sum(new_residual * new_residual, axis=0), ("tm", "nin"))
    new_direction = new_residual + (new_norm / (old_norm + NORM_EPS))[None, :] * direction
    return (new_iterate, new_residual, new_direction)


def solution(mesh):
    in_specs = (
        P("tm", "nin"),
        P("tm"),
        P("nin", "nout"),
        P(("nin", "tm"), "nout"),
        P(("nin", "tm"), "nout"),
        P(("nin", "tm"), "nout"),
    )
    out_specs = (P(("nin", "tm"), "nout"), P(("nin", "tm"), "nout"), P(("nin", "tm"), "nout"))
    return jax.shard_map(
        per_device, mesh=mesh, in_specs=in_specs, out_specs=out_specs, check_vma=False
    )
```

profile of v0, /device:TPU:2, one launch (start us, length us, event | category | flops | bytes accessed | tf_op | source)
XLA Modules:
  0.0 800.1 jit_solution(18235166921538115580)
XLA Ops:
  7.2 0.0 copy-start
  7.2 0.0 all-gather.2.cloned.1.call-start
  7.2 1.8 convert_element_type.56
  9.0 0.0 all-gather.2.cloned.1.call-update
  9.0 0.0 all-reduce.4.cloned.1.call-start
  9.1 0.2 multiply_reduce_fusion.3
  9.3 0.1 divide_convert_fusion
  9.4 0.1 copy.17
  9.6 0.1 bitcast_clamp_fusion
  9.7 57.8 %gather_fusion.1 = bf16[16384,8]{1,0:T(8,128)(2,1)} fusion(bf16[8,128]{0,1:T(8,128)(2,1)S(1)} %copy.17, s32[16384]{0:T(1024)S(1)} %bitcast_clamp_fusion), kind=kCustom, calls=%fused_computation.1.clone | custom fusion | bytes 589824 | tf_op jit(solution)/shard_map/jit(_take)/gather | solution.py:40
  67.5 0.0 copy-start.5
  67.5 3.6 copy.20
  71.2 0.0 copy-done.5
  71.2 0.1 fusion.30
  71.3 1.1 fusion.1
  72.4 1.8 collective-permute-start
  74.2 57.8 %gather_fusion = bf16[16384,8]{1,0:T(8,128)(2,1)} fusion(bf16[8,128]{0,1:T(8,128)(2,1)S(1)} %copy.17, s32[16384]{0:T(1024)S(1)} %bitcast_clamp_fusion.1), kind=kCustom, calls=%fused_computation.clone | custom fusion | bytes 589824 | tf_op jit(solution)/shard_map/jit(_take)/gather | solution.py:40
  132.0 3.6 copy.18
  135.6 0.1 fusion.27
  135.7 0.3 convolution_bitcast_fusion
  136.0 0.0 collective-permute-done
  136.0 0.1 bitcast_convert_fusion
  136.1 0.4 fusion
  136.5 2.1 copy.21
  138.6 0.0 copy-done
  138.6 0.0 copy-start.2
  138.6 2.8 convolution_convert_fusion.3
  141.4 0.0 all-gather.2.cloned.1.call-done
  141.4 0.0 copy-done.2
  141.4 3.0 convolution_convert_fusion.2
  144.4 0.0 all-reduce.4.cloned.1.call-update
  144.5 0.0 reduce-scatter.2.cloned.1.call-start
  144.5 0.0 copy-done.7
  144.5 85.0 %all-reduce.4.cloned.1.call-done = (bf16[256,512]{1,0:T(8,128)(2,1)}, bf16[256,512]{1,0:T(8,128)(2,1)}) async-done(((bf16[256,512]{1,0:T(8,128)(2,1)}, bf16[256,512]{1,0:T(8,128)(2,1)}), (bf16[256,512]{1,0:T(8,128)(2,1)}, bf16[256,512]{1,0:T(8,128)(2,1)})) %all-reduce.4.cloned.1.call-update) | async-done | bytes 524304 | tf_op jit(solution)/shard_map/psum | solution.py:74
  229.5 0.0 copy-start.4
  229.5 3.2 convolution_convert_fusion
  232.8 0.0 copy-start.1
  232.8 0.0 reduce-scatter.2.cloned.1.call-update
  232.8 0.0 copy-done.4
  232.9 59.8 %reduce-scatter.2.cloned.1.call-done = bf16[128,512]{1,0:T(8,128)(2,1)} async-done(((bf16[2048,512]{1,0:T(8,128)(2,1)}), bf16[128,512]{1,0:T(8,128)(2,1)}) %reduce-scatter.2.cloned.1.call-update) | async-done | bytes 131088 | tf_op jit(solution)/shard_map/reduce_scatter | solution.py:78
  292.7 0.0 copy-done.1
  292.7 1.0 multiply_reduce_fusion.1
  293.6 250.6 %all-reduce = (f32[512]{0:T(512)S(1)}, f32[512]{0:T(512)S(1)}) all-reduce(f32[512]{0:T(512)S(1)} %multiply_reduce_fusion.2, f32[512]{0:T(512)S(1)} %multiply_reduce_fusion.1), channel_id=1, replica_groups=mesh['tm'=16,'nin'=8,'nout'=4] {'tm','nin'}, use_global_device_ids=true, to_apply=%region_1.2 | all-reduce | flops 1024 | bytes 8192 | tf_op jit(solution)/shard_map/psum | solution.py:88
  544.3 0.0 copy-done.6
  544.3 1.7 multiply_reduce_fusion
  546.0 246.8 %psum.39 = f32[512]{0:T(512)S(1)} all-reduce(f32[512]{0:T(512)S(1)} %get-tuple-element.8), channel_id=1, replica_groups=mesh['tm'=16,'nin'=8,'nout'=4] {'tm','nin'}, use_global_device_ids=true, to_apply=%region_9.11 | all-reduce | flops 512 | bytes 4096 | tf_op jit(solution)/shard_map/psum | solution.py:95
  792.8 0.8 multiply_add_fusion
  793.5 0.0 copy-done.3
  (12 shorter events, 0.1 us)
Async XLA Ops:
  7.2 131.5 %copy-start = (bf16[2048,512]{1,0:T(8,128)(2,1)S(1)}, bf16[2048,512]{1,0:T(8,128)(2,1)}, u32[]{:S(2)}) copy-start(bf16[2048,512]{1,0:T(8,128)(2,1)} %param.10) | copy-start | bytes 6291460
  7.2 134.2 %all-gather.2.cloned.1.call-start = ((), (), s32[]{:S(2)}) async-start(), calls=%async_computation.1 | async-start | bytes 2228224 | tf_op jit(solution)/shard_map/all_gather | solution.py:67
  9.0 220.5 %all-reduce.4.cloned.1.call-start = ((), (), s32[]{:S(2)}) async-start(), calls=%async_computation.3 | async-start | bytes 1048576 | tf_op jit(solution)/shard_map/psum | solution.py:74
  67.5 3.6 copy-start.5
  72.4 63.6 %collective-permute-start = (bf16[128,256,8]{1,0,2:T(8,128)(2,1)}, bf16[128,256,8]{1,0,2:T(8,128)(2,1)S(1)}, u32[]{:S(2)}, u32[]{:S(2)}) collective-permute-start(bf16[128,256,8]{1,0,2:T(8,128)(2,1)} %fusion.1), channel_id=1, source_target_pairs={{0,32},{32,64},{64,96},{96,128},{128,160},{160,192},{192,224},{224... | collective-permute-start | bytes 1572872 | tf_op jit(solution)/shard_map/ppermute | solution.py:16
  138.6 2.8 copy-start.2
  141.4 3.1 copy-start.7
  144.5 148.2 %reduce-scatter.2.cloned.1.call-start = ((), (), s32[]{:S(2)}) async-start(), calls=%async_computation.2 | async-start | bytes 2228224 | tf_op jit(solution)/shard_map/reduce_scatter | solution.py:78
  229.5 3.3 copy-start.4
  232.8 59.9 %copy-start.1 = (f32[128,512]{1,0:T(8,128)S(1)}, f32[128,512]{1,0:T(8,128)}, u32[]{:S(2)}) copy-start(f32[128,512]{1,0:T(8,128)} %param.11) | copy-start | bytes 786436
  232.8 311.5 %copy-start.6 = (f32[128,512]{1,0:T(8,128)S(1)}, f32[128,512]{1,0:T(8,128)}, u32[]{:S(2)}) copy-start(f32[128,512]{1,0:T(8,128)} %param.13) | copy-start | bytes 786436
  546.0 247.6 %copy-start.3 = (f32[128,512]{1,0:T(8,128)}, f32[128,512]{1,0:T(8,128)S(1)}, u32[]{:S(2)}) copy-start(f32[128,512]{1,0:T(8,128)S(1)} %get-tuple-element.9) | copy-start | bytes 786436
Sparse Core Ops, SparseCore 0:
  10.7 46.5 all-gather.1
  144.6 84.9 all-reduce.3
  232.9 59.6 reduce-scatter.1
where the time goes:
time: 800 us
  blocking collectives  497 us (62%)
  waiting for transfers between devices  145 us (18%)
  local copies, waits for them, and re-layouts  125 us (16%)
  between operations  13.9 us (2%)
  matrix products  10.8 us (1%)
    psum x1, blocking collectives, per_device(): lax.psum((jnp.sum(residual * residual, axis=0), jnp.sum(direction * curva...  251 us
    psum x1, blocking collectives, per_device(): lax.psum(jnp.sum(new_residual * new_residual, axis=0), ('tm', 'nin'))  247 us
    gather x4, local copies, waits for them, and re-layouts, lag_kernel(): jnp.take(basis_rows.T, take_index, axis=1)  123 us
    psum x1, waiting for transfers between devices, per_device(): lax.psum(along_part.astype(jnp.bfloat16), 'nin').astype(jnp.float32)  85 us
    reduce_scatter x1, waiting for transfers between devices, per_device(): lax.psum_scatter(lax.dot_general(columns, weighted, (((0,), (0,)), ((), (...  59.8 us
  transfers between devices with their start and end apart: 4, of which 2 were waited for; matrix products, arithmetic and copies ran while one was open for 16% of the time, Pallas kernels for 0%

commit v1 on v0

--- a/solution.py
+++ b/solution.py
@@ -92,7 +92,9 @@
     step_size = old_norm / curvature
     new_iterate = iterate + step_size[None, :] * direction
     new_residual = residual - step_size[None, :] * curvature_prod
-    new_norm = lax.psum(jnp.sum(new_residual * new_residual, axis=0), ("tm", "nin"))
+    own = jnp.sum(new_residual * new_residual, axis=0)
+    terms = lax.all_gather(own, ("tm", "nin"))
+    new_norm = jnp.sum(terms, axis=0)
     new_direction = new_residual + (new_norm / (old_norm + NORM_EPS))[None, :] * direction
     return (new_iterate, new_residual, new_direction)
 

time: 800 us -> 643 us (0.80)
  the two profiles are of different devices: /device:TPU:2 before, /device:TPU:27 now
where the time goes in v1:
time: 643 us
  blocking collectives  340 us (53%)
  waiting for transfers between devices  142 us (22%)
  local copies, waits for them, and re-layouts  125 us (19%)
  between operations  13.9 us (2%)
  matrix products  10.8 us (2%)
    psum x1, blocking collectives, per_device(): lax.psum((jnp.sum(residual * residual, axis=0), jnp.sum(direction * curva...  236 us
    gather x4, local copies, waits for them, and re-layouts, lag_kernel(): jnp.take(basis_rows.T, take_index, axis=1)  123 us
    all_gather x1, blocking collectives, per_device(): terms = lax.all_gather(own, ('tm', 'nin'))  104 us
    psum x1, waiting for transfers between devices, per_device(): lax.psum(along_part.astype(jnp.bfloat16), 'nin').astype(jnp.float32)  77.2 us
    reduce_scatter x1, waiting for transfers between devices, per_device(): lax.psum_scatter(lax.dot_general(columns, weighted, (((0,), (0,)), ((), (...  64.4 us
  transfers between devices with their start and end apart: 4, of which 2 were waited for; matrix products, arithmetic and copies ran while one was open for 20% of the time, Pallas kernels for 0%

profile of v1, /device:TPU:27, one launch (start us, length us, event | category | flops | bytes accessed | tf_op | source)
XLA Modules:
  0.0 642.5 jit_solution(2034350802071964556)
XLA Ops:
  7.2 0.0 copy-start
  7.2 0.0 all-gather.4.cloned.1.call-start
  7.2 1.8 convert_element_type.56
  9.0 0.0 all-gather.4.cloned.1.call-update
  9.0 0.0 all-reduce.4.cloned.1.call-start
  9.1 0.2 multiply_reduce_fusion.3
  9.3 0.1 divide_convert_fusion
  9.4 0.1 copy.20
  9.6 0.1 bitcast_clamp_fusion
  9.7 57.8 %gather_fusion.1 = bf16[16384,8]{1,0:T(8,128)(2,1)} fusion(bf16[8,128]{0,1:T(8,128)(2,1)S(1)} %copy.20, s32[16384]{0:T(1024)S(1)} %bitcast_clamp_fusion), kind=kCustom, calls=%fused_computation.1.clone | custom fusion | bytes 589824 | tf_op jit(solution)/shard_map/jit(_take)/gather | solution.py:40
  67.5 0.0 copy-start.5
  67.5 3.6 copy.23
  71.2 0.0 copy-done.5
  71.2 0.1 fusion.30
  71.3 1.1 fusion.1
  72.4 5.0 collective-permute-start
  77.4 57.8 %gather_fusion = bf16[16384,8]{1,0:T(8,128)(2,1)} fusion(bf16[8,128]{0,1:T(8,128)(2,1)S(1)} %copy.20, s32[16384]{0:T(1024)S(1)} %bitcast_clamp_fusion.1), kind=kCustom, calls=%fused_computation.clone | custom fusion | bytes 589824 | tf_op jit(solution)/shard_map/jit(_take)/gather | solution.py:40
  135.2 3.6 copy.21
  138.8 0.1 fusion.27
  138.9 0.3 convolution_bitcast_fusion
  139.2 0.0 collective-permute-done
  139.2 0.1 bitcast_convert_fusion
  139.3 0.4 fusion
  139.7 2.1 copy.24
  141.8 0.0 copy-done
  141.8 2.8 convolution_convert_fusion.3
  144.6 0.0 copy-start.7
  144.6 0.0 all-gather.4.cloned.1.call-done
  144.6 0.0 copy-done.2
  144.6 3.1 convolution_convert_fusion.2
  147.6 0.0 all-reduce.4.cloned.1.call-update
  147.7 0.0 reduce-scatter.2.cloned.1.call-start
  147.7 0.0 copy-done.7
  147.7 77.2 %all-reduce.4.cloned.1.call-done = (bf16[256,512]{1,0:T(8,128)(2,1)}, bf16[256,512]{1,0:T(8,128)(2,1)}) async-done(((bf16[256,512]{1,0:T(8,128)(2,1)}, bf16[256,512]{1,0:T(8,128)(2,1)}), (bf16[256,512]{1,0:T(8,128)(2,1)}, bf16[256,512]{1,0:T(8,128)(2,1)})) %all-reduce.4.cloned.1.call-update) | async-done | bytes 524304 | tf_op jit(solution)/shard_map/psum | solution.py:74
  224.9 0.0 copy-start.4
  224.9 3.2 convolution_convert_fusion
  228.2 0.0 reduce-scatter.2.cloned.1.call-update
  228.2 0.0 copy-done.4
  228.2 64.4 %reduce-scatter.2.cloned.1.call-done = bf16[128,512]{1,0:T(8,128)(2,1)} async-done(((bf16[2048,512]{1,0:T(8,128)(2,1)}), bf16[128,512]{1,0:T(8,128)(2,1)}) %reduce-scatter.2.cloned.1.call-update) | async-done | bytes 131088 | tf_op jit(solution)/shard_map/reduce_scatter | solution.py:78
  292.7 0.0 copy-done.1
  292.7 1.0 multiply_reduce_fusion.1
  293.6 235.6 %all-reduce = (f32[512]{0:T(512)S(1)}, f32[512]{0:T(512)S(1)}) all-reduce(f32[512]{0:T(512)S(1)} %multiply_reduce_fusion.2, f32[512]{0:T(512)S(1)} %multiply_reduce_fusion.1), channel_id=1, replica_groups=mesh['tm'=16,'nin'=8,'nout'=4] {'tm','nin'}, use_global_device_ids=true, to_apply=%region_1.2 | all-reduce | flops 1024 | bytes 8192 | tf_op jit(solution)/shard_map/psum | solution.py:88
  529.3 0.0 copy-done.6
  529.3 1.7 multiply_reduce_fusion
  531.0 104.1 %all-gather.1 = f32[128,1,512]{2,1,0:T(1,128)S(1)} all-gather(f32[1,1,512]{2,1,0:T(1,128)S(1)} %bitcast.63), channel_id=2, replica_groups=mesh['tm'=16,'nin'=8,'nout'=4] {'tm','nin'}, dimensions={0}, use_global_device_ids=true | all-gather | bytes 264192 | tf_op jit(solution)/shard_map/all_gather | solution.py:96
  635.0 0.2 reduce_sum.49
  635.3 0.8 multiply_add_fusion
  636.0 0.0 copy-done.3
  (13 shorter events, 0.1 us)
Async XLA Ops:
  7.2 134.7 %copy-start = (bf16[2048,512]{1,0:T(8,128)(2,1)S(1)}, bf16[2048,512]{1,0:T(8,128)(2,1)}, u32[]{:S(2)}) copy-start(bf16[2048,512]{1,0:T(8,128)(2,1)} %param.10) | copy-start | bytes 6291460
  7.2 137.4 %all-gather.4.cloned.1.call-start = ((), (), s32[]{:S(2)}) async-start(), calls=%async_computation.1 | async-start | bytes 2228224 | tf_op jit(solution)/shard_map/all_gather | solution.py:67
  9.0 215.9 %all-reduce.4.cloned.1.call-start = ((), (), s32[]{:S(2)}) async-start(), calls=%async_computation.3 | async-start | bytes 1048576 | tf_op jit(solution)/shard_map/psum | solution.py:74
  67.5 3.6 copy-start.5
  72.4 66.8 %collective-permute-start = (bf16[128,256,8]{1,0,2:T(8,128)(2,1)}, bf16[128,256,8]{1,0,2:T(8,128)(2,1)S(1)}, u32[]{:S(2)}, u32[]{:S(2)}) collective-permute-start(bf16[128,256,8]{1,0,2:T(8,128)(2,1)} %fusion.1), channel_id=1, source_target_pairs={{0,32},{32,64},{64,96},{96,128},{128,160},{160,192},{192,224},{224... | collective-permute-start | bytes 1572872 | tf_op jit(solution)/shard_map/ppermute | solution.py:16
  141.8 2.8 copy-start.2
  144.6 3.1 copy-start.7
  147.7 145.0 %reduce-scatter.2.cloned.1.call-start = ((), (), s32[]{:S(2)}) async-start(), calls=%async_computation.2 | async-start | bytes 2228224 | tf_op jit(solution)/shard_map/reduce_scatter | solution.py:78
  224.9 3.3 copy-start.4
  228.2 64.5 %copy-start.1 = (f32[128,512]{1,0:T(8,128)S(1)}, f32[128,512]{1,0:T(8,128)}, u32[]{:S(2)}) copy-start(f32[128,512]{1,0:T(8,128)} %param.11) | copy-start | bytes 786436
  228.2 301.1 %copy-start.6 = (f32[128,512]{1,0:T(8,128)S(1)}, f32[128,512]{1,0:T(8,128)}, u32[]{:S(2)}) copy-start(f32[128,512]{1,0:T(8,128)} %param.13) | copy-start | bytes 786436
  531.0 105.1 %copy-start.3 = (f32[128,512]{1,0:T(8,128)}, f32[128,512]{1,0:T(8,128)S(1)}, u32[]{:S(2)}) copy-start(f32[128,512]{1,0:T(8,128)S(1)} %get-tuple-element.9) | copy-start | bytes 786436
Sparse Core Ops, SparseCore 0:
  10.7 46.3 all-gather.3
  147.8 77.0 all-reduce.3
  228.3 64.3 reduce-scatter.1
